TPU v7x, 128 devices: a whole 4x4x4 slice. The times are simulated.
128 devices in a mesh: dom: 32 (over x, y, z_hi), orb: 4 (over z_lo, core).
Axes of the slice: x: 4, y: 4, z: 4 (z_hi: 2, z_lo: 2; z = z_hi * 2 + z_lo), core: 2. Of those that a mesh axis runs over, the one named last changes fastest.
Arguments:
- block: float32 [16, 384, 32, 128], P('orb', 'dom'), may hold values from -6 to 6
- potential: float32 [384, 32, 128], P('dom'), may hold values from -1.5 to 0.5
- stored: bfloat16 [256, 384, 32, 128], P('orb', 'dom'), may hold values from -0.0048828125 to 0.0048828125
Outputs:
- filtered: float32 [16, 384, 32, 128], P('orb', 'dom')
- intersection: float32 [256, 16], P('orb')
All inputs are finite; a program needn't handle non-finite values.
Results may differ from a plain program's by a relative error of at most 0.0029.
Values may be sent and summed in bfloat16 or wider, within the bound.
A program may use at most 256 MiB of HBM per device.

v0:
```python
import jax
import jax.numpy as jnp
import ml_dtypes
import numpy as np
from jax import lax
from jax.experimental import pallas as pl
from jax.experimental.pallas import tpu as pltpu
from jax.sharding import PartitionSpec as P

F32, BF16 = jnp.float32, jnp.bfloat16
MESH = pl.DeviceIdType.MESH

coeffs = (
    -5369.0 / 1800.0,
    12.0 / 7.0,
    -15.0 / 56.0,
    10.0 / 189.0,
    -1.0 / 112.0,
    2.0 / 825.0,
    -1.0 / 5544.0,
)
WEIGHTS = tuple(-0.5 * 6.25 * c / 16.0 for c in coeffs)
SHIFT = (-0.5 * 6.25 * 3.0 * coeffs[0] - 36.0) / 16.0
CX, NY, NZ = 12, 32, 128
PAIRS, SLABS = 16, 32


HIGHS = tuple(float(np.float32(w).astype(ml_dtypes.bfloat16)) for w in WEIGHTS)
LOWS = tuple(w - high for w, high in zip(WEIGHTS, HIGHS))


def iotas(shape):
    return lax.broadcasted_iota(jnp.int32, shape, 0), lax.broadcasted_iota(jnp.int32, shape, 1)


def circulant(n, values):
    i, j = iotas((n, n))
    distance = (i - j) & (n - 1)
    matrix = jnp.zeros((n, n), F32)
    for m in range(1, 7):
        matrix = jnp.where((distance == m) | (distance == n - m), values[m], matrix)
    return matrix


def kernel(
    block, potential, stored, filtered, inter,
    cz_ref, cy_ref, blkf, potf, st, blkb, rb, potb, diag, a0, a1, a2, a3, a4, sendp, low, outf, acc, part, ar1, ar2,
    local_sem, send_sem, recv_sem,
):
    dom, orb = lax.axis_index("dom"), lax.axis_index("orb")
    h = lax.rem(dom, 2)
    pair = dom // 2
    up, down = lax.rem(dom + 2, SLABS), lax.rem(dom + SLABS - 2, SLABS)
    partner = dom + 1 - 2 * h
    core = lax.rem(orb, 2)
    sibling = orb + 1 - 2 * core
    across = lax.rem(orb + 2, 4)
    row, column = lax.rem(dom, 8), dom // 8

    def rowpeer(k):
        return column * 8 + lax.rem(row + k, 8)

    def columnpeer(k):
        return lax.rem(column + k, 4) * 8 + row

    barrier = pltpu.get_barrier_semaphore()
    peers = [(partner, orb), (up, orb), (down, orb), (dom, sibling), (dom, across), (partner, across)]
    peers += [(rowpeer(k), orb) for k in range(1, 8)] + [(columnpeer(k), orb) for k in range(1, 4)]
    for peer in peers:
        pl.semaphore_signal(barrier, inc=1, device_id=peer, device_id_type=MESH)

    other = 1 - h
    order = (2 * other, 2 * other + 1, 2 * h, 2 * h + 1)
    loads = [pltpu.make_async_copy(block.at[i], blkf.at[i], local_sem.at[n]) for n, i in enumerate(order)]
    loads.insert(2, pltpu.make_async_copy(potential, potf, local_sem.at[4]))
    load_stored = pltpu.make_async_copy(stored, st, local_sem.at[5])
    for load in loads:
        load.start()
    high, rest = circulant(NZ, HIGHS), circulant(NZ, LOWS)
    cz_ref[...] = jnp.concatenate([jnp.concatenate([high, rest], 1)] * 2, 0).astype(BF16)
    high, rest = circulant(NY, HIGHS), circulant(NY, LOWS)
    cy_ref[...] = jnp.concatenate([jnp.concatenate([high, high], 1), jnp.concatenate([rest, rest], 1)], 0).astype(BF16)
    for load in loads:
        load.wait()
    load_stored.start()
    for i in range(4):
        blkb[i] = blkf[i].astype(BF16)
    for r in range(2):
        potb[r, pl.ds(24 + 12 * h, 12)] = potf[:, 16 * r : 16 * r + 16].astype(BF16)

    pl.semaphore_wait(barrier, len(peers))

    def remote(i, src, dst, peer):
        return pltpu.make_async_remote_copy(
            src_ref=src, dst_ref=dst, send_sem=send_sem.at[i], recv_sem=recv_sem.at[i],
            device_id=peer, device_id_type=MESH,
        )

    def swap(o):
        return (remote(o, blkb.at[2 * other + o], rb.at[o, 2 + h], (partner, orb)),)

    def own(o):
        src = blkb.at[2 * h + o]
        return remote(2 + o, src, rb.at[o, h], (up, orb)), remote(4 + o, src, rb.at[o, 4 + h], (down, orb))

    def forward(o):
        src = rb.at[o, 2 + other]
        return remote(6 + o, src, rb.at[o, other], (up, orb)), remote(8 + o, src, rb.at[o, 4 + other], (down, orb))

    group_low = 4 * orb + 2 * h

    def gather(o):
        here = low.at[group_low + o]
        return (
            remote(10 + o, sendp.at[o], here, (partner, orb)),
            remote(12 + o, sendp.at[o], here, (partner, across)),
            remote(14 + o, here, here, (dom, across)),
            remote(16 + o, here, here, (dom, sibling)),
        )

    def relay(o):
        arrived = (4 * orb + 2 * other + o, 4 * across + 2 * other + o, 4 * across + 2 * h + o)
        return tuple(remote(18 + 2 * n + o, low.at[i], low.at[i], (dom, sibling)) for n, i in enumerate(arrived))

    def pot_copy(i, src, dst, length, peer):
        return remote(i, potb.at[core, pl.ds(src, length)], potb.at[core, pl.ds(dst, length)], peer)

    def pot_copies(i, kind):
        src = 24 + 12 * kind
        rest = 6 * (1 - kind)
        return (
            pot_copy(i, src + 6, 12 * kind + 6, 6, (up, orb)),
            pot_copy(i + 1, src, 48 + 12 * kind, 6, (down, orb)),
            pot_copy(i + 2, src + rest, 48 - 36 * kind + rest, 6, (lax.select(kind == 1, up, down), orb)),
        )

    swap_pot = (pot_copy(24, 24 + 12 * h, 24 + 12 * h, 12, (partner, orb)),)
    own_pot, forward_pot = pot_copies(25, h), pot_copies(28, other)
    share_pot = tuple(
        pot_copy(31 + n, at, at, length, (dom, sibling))
        for n, (at, length) in enumerate(((6, 18), (24 + 12 * other, 12), (48, 18)))
    )

    def start(copies):
        for copy in copies:
            copy.start()

    def received(copies):
        for copy in copies:
            copy.wait_recv()

    def sent(copies):
        for copy in copies:
            copy.wait_send()

    start(swap(0) + own(0) + swap_pot + own_pot + swap(1) + own(1))
    received(swap(0))
    start(forward(0))
    received(swap_pot)
    start(forward_pot)
    received(swap(1))
    start(forward(1))

    in_low = jnp.where(pair > 0, 1.0, 0.0).astype(F32)
    in_high = jnp.where(pair < PAIRS - 1, 1.0, 0.0).astype(F32)

    received(own_pot + forward_pot)
    start(share_pot)
    received(share_pot)
    for r in range(2):
        diag[:, 16 * r : 16 * r + 16] = potb[r, 6:66].astype(F32) * (1.0 / 16.0) + SHIFT
    diag[pl.ds(18 + 12 * h, 12)] = potf[...] * (1.0 / 16.0) + SHIFT

    def step(src, src_at, prev, prev_at, dst, dst_at, groups):
        for e in range(dst_at, dst_at + 12 * groups, 12):
            s = e - src_at
            v = src[s : s + 12].reshape(12 * NY, NZ)
            high = v.astype(BF16)
            rest = (v - high.astype(F32)).astype(BF16)
            along_z = jnp.dot(jnp.concatenate([high, rest], 1), cz_ref[...], preferred_element_type=F32)
            along_z = along_z[:, :NZ] + along_z[:, NZ:]
            along_y = []
            for i in range(0, 12, 2):
                parts = [
                    jnp.concatenate([a[NY * k : NY * k + NY] for a in (high, rest)], 0) for k in (i, i + 1)
                ]
                product = jnp.dot(cy_ref[...], jnp.concatenate(parts, 1), preferred_element_type=F32)
                product = product[:NY] + product[NY:]
                along_y += [product[:, :NZ], product[:, NZ:]]
            for y in range(0, NY, 8):
                window = [src[s - 6 + k, y : y + 8] for k in range(24)]
                for i in range(12):
                    t = window[6 + i] * diag[e + i - 6, y : y + 8]
                    t = t + (along_z[NY * i + y : NY * i + y + 8] + along_y[i][y : y + 8])
                    for m in range(1, 7):
                        t = t + WEIGHTS[m] * (window[6 + i + m] + window[6 + i - m])
                    if prev is None:
                        t = t * 0.5
                    else:
                        t = t - prev[e + i - prev_at, y : y + 8]
                    if e + i < 24:
                        t = t * in_low
                    elif e + i >= 48:
                        t = t * in_high
                    dst[e + i - dst_at, y : y + 8] = t

    def out_own(o):
        return pltpu.make_async_copy(a4.at[o, pl.ds(12 * h, 12)], filtered.at[2 * h + o], local_sem.at[6 + o])

    def out_other(o):
        return pltpu.make_async_copy(outf.at[o], filtered.at[2 * other + o], local_sem.at[8 + o])

    def orbital(o, carry):
        received(own(o) + forward(o))
        for slab in (0, 1, 4, 5):
            a0[12 * slab : 12 * slab + 12] = rb[o, slab].astype(F32) * (in_low if slab < 2 else in_high)
        a0[pl.ds(24 + 12 * other, 12)] = rb[o, 2 + other].astype(F32)
        a0[pl.ds(24 + 12 * h, 12)] = blkf[2 * h + o]
        step(a0, 0, None, 0, a1, 6, 5)
        step(a1, 6, a0, 0, a2, 12, 4)
        step(a2, 12, a1, 6, a3, 18, 3)
        step(a3, 18, a2, 12, a4.at[o], 24, 2)
        sendp[o] = a4[o, pl.ds(12 * other, 12)].astype(BF16)
        start(gather(o)[:2])
        low[group_low + o] = a4[o, pl.ds(12 * h, 12)].astype(BF16)
        start(gather(o)[2:])
        out_own(o).start()
        return carry

    lax.fori_loop(0, 2, orbital, 0)

    for o in range(2):
        for i in (2, 1, 0):
            received(gather(o)[i : i + 1])
            start(relay(o)[i : i + 1])
        outf[o] = low[4 * orb + 2 * other + o].astype(F32)
        out_other(o).start()
    for o in range(2):
        received(gather(o)[3:] + relay(o))

    load_stored.wait()
    total = None
    for p in range(0, 12, 2):
        for y in range(0, NY, 16):
            left = [st[:, p + i, y : y + 16].reshape(1024, NZ) for i in range(2)]
            right = [low[:, p + i, y : y + 16].reshape(256, NZ) for i in range(2)]
            term = lax.dot_general(
                jnp.concatenate(left, 1), jnp.concatenate(right, 1), (((1,), (1,)), ((), ())), preferred_element_type=F32
            )
            total = term if total is None else total + term
    acc[...] = total
    i, j = iotas((16, 256))
    same = i == j % 16
    rows = jnp.sum(jnp.where(same[None], acc[...].reshape(64, 16, 256), 0.0), axis=1)
    first = rows.astype(BF16)
    rest = rows - first.astype(F32)
    second = rest.astype(BF16)
    third = (rest - second.astype(F32)).astype(BF16)
    i, j = iotas((16, 256))
    fold = jnp.where(i == j // 16, 1.0, 0.0).astype(BF16)
    total = jnp.zeros((16, 64), F32)
    for piece in (third, second, first):
        total = total + lax.dot_general(fold, piece, (((1,), (1,)), ((), ())), preferred_element_type=F32)

    for buffer, size, me, peer in ((ar1, 8, row, rowpeer), (ar2, 4, column, columnpeer)):
        part_at = part.at[0 if size == 8 else 1]
        part_at[...] = total
        buffer[me] = total
        at = 33 if size == 8 else 40
        copies = [remote(at + k, part_at, buffer.at[me], (peer(k), orb)) for k in range(1, size)]
        start(copies)
        received(copies)
        total = buffer[0]
        for k in range(1, size):
            total = total + buffer[k]
        sent(copies)
    inter[...] = total

    sent(swap_pot + own_pot + forward_pot + share_pot)
    for o in range(2):
        sent(swap(o) + own(o) + forward(o) + gather(o) + relay(o))
        out_own(o).wait()
        out_other(o).wait()


def body(block, potential, stored):
    planes = (CX, NY, NZ)
    vmem, anywhere = pl.BlockSpec(memory_space=pltpu.VMEM), pl.BlockSpec(memory_space=pl.ANY)
    filtered, inter = pl.pallas_call(
        kernel,
        out_shape=(jax.ShapeDtypeStruct((4,) + planes, F32), jax.ShapeDtypeStruct((16, 64), F32)),
        in_specs=[anywhere] * 3,
        out_specs=(anywhere, vmem),
        scratch_shapes=[
            pltpu.VMEM((256, 256), BF16),
            pltpu.VMEM((64, 64), BF16),
            pltpu.VMEM((4,) + planes, F32),
            pltpu.VMEM(planes, F32),
            pltpu.VMEM((64,) + planes, BF16),
            pltpu.VMEM((4,) + planes, BF16),
            pltpu.VMEM((2, 6) + planes, BF16),
            pltpu.VMEM((2, 72, 16, NZ), BF16),
            pltpu.VMEM((60, NY, NZ), F32),
            pltpu.VMEM((72, NY, NZ), F32),
            pltpu.VMEM((60, NY, NZ), F32),
            pltpu.VMEM((48, NY, NZ), F32),
            pltpu.VMEM((36, NY, NZ), F32),
            pltpu.VMEM((2, 24, NY, NZ), F32),
            pltpu.VMEM((2,) + planes, BF16),
            pltpu.VMEM((16,) + planes, BF16),
            pltpu.VMEM((2,) + planes, F32),
            pltpu.VMEM((1024, 256), F32),
            pltpu.VMEM((2, 16, 64), F32),
            pltpu.VMEM((8, 16, 64), F32),
            pltpu.VMEM((4, 16, 64), F32),
            pltpu.SemaphoreType.DMA((10,)),
            pltpu.SemaphoreType.DMA((44,)),
            pltpu.SemaphoreType.DMA((44,)),
        ],
        compiler_params=pltpu.CompilerParams(collective_id=0, has_side_effects=True, vmem_limit_bytes=60 * 2**20),
    )(block, potential, stored)
    return filtered, inter.T


def solution(mesh):
    in_specs = (P("orb", "dom", None, None), P("dom", None, None), P("orb", "dom", None, None))
    out_specs = (P("orb", "dom", None, None), P("orb", None))
    return jax.shard_map(body, mesh=mesh, in_specs=in_specs, out_specs=out_specs, check_vma=False)
```

profile of v0, /device:TPU:0, one launch (start us, length us, event | category | flops | bytes accessed | tf_op | source)
XLA Modules:
  0.0 51.6 jit_solution(1900189261315594600)
XLA Ops:
  0.6 47.6 %shard_map.50 = (f32[4,12,32,128]{3,2,1,0:T(8,128)}, f32[16,64]{1,0:T(8,128)}) custom-call(f32[4,12,32,128]{3,2,1,0:T(8,128)} %block.1, f32[12,32,128]{2,1,0:T(8,128)} %potential.1, bf16[64,12,32,128]{3,2,1,0:T(8,128)(2,1)} %stored.1), custom_call_target="tpu_custom_call" | custom-call | tf_op jit(solution)/shard_map/pallas_call | solution.py:289
  48.3 2.1 %copy.7 = f32[4,12,32,128]{3,2,1,0:T(8,128)} copy(f32[4,12,32,128]{3,2,1,0:T(8,128)} %get-tuple-element.8) | data formatting | bytes 1572864
  50.3 1.3 %copy.8 = f32[64,16]{0,1:T(8,128)} copy(f32[64,16]{0,1:T(8,128)} %bitcast.1) | data formatting | bytes 8192
where the time goes:
time: 51.9 us; the launch traced here: 51.6 us
  Pallas kernels  47.6 us (92%)
  local copies, waits for them, and re-layouts  3.36 us (6%)
  between operations  0.64 us (1%)
    pallas_call x1, Pallas kernels, body(): pl.pallas_call(kernel, out_shape=(jax.ShapeDtypeStruct((4,) + planes, F32...  47.6 us
    unnamed x2, local copies, waits for them, and re-layouts  3.36 us

commit v1 on v0

--- a/solution.py
+++ b/solution.py
@@ -64,8 +64,8 @@
         return lax.rem(column + k, 4) * 8 + row
 
     barrier = pltpu.get_barrier_semaphore()
-    peers = [(partner, orb), (up, orb), (down, orb), (dom, sibling), (dom, across), (partner, across)]
-    peers += [(rowpeer(k), orb) for k in range(1, 8)] + [(columnpeer(k), orb) for k in range(1, 4)]
+    peers = [(rowpeer(k), orb) for k in (1, 7)] + [(up, orb), (down, orb), (dom, sibling), (dom, across), (partner, across)]
+    peers += [(rowpeer(k), orb) for k in range(2, 7)] + [(columnpeer(k), orb) for k in range(1, 4)]
     for peer in peers:
         pl.semaphore_signal(barrier, inc=1, device_id=peer, device_id_type=MESH)
 
@@ -153,11 +153,11 @@
         for copy in copies:
             copy.wait_send()
 
-    start(swap(0) + own(0) + swap_pot + own_pot + swap(1) + own(1))
+    start(swap_pot + own_pot + swap(0) + own(0))
+    received(swap_pot)
+    start(forward_pot + swap(1))
     received(swap(0))
-    start(forward(0))
-    received(swap_pot)
-    start(forward_pot)
+    start(forward(0) + own(1))
     received(swap(1))
     start(forward(1))
 
@@ -171,36 +171,34 @@
         diag[:, 16 * r : 16 * r + 16] = potb[r, 6:66].astype(F32) * (1.0 / 16.0) + SHIFT
     diag[pl.ds(18 + 12 * h, 12)] = potf[...] * (1.0 / 16.0) + SHIFT
 
-    def step(src, src_at, prev, prev_at, dst, dst_at, groups):
-        for e in range(dst_at, dst_at + 12 * groups, 12):
+    def step(src, src_at, prev, prev_at, dst, dst_at, starts, masked=True):
+        for e in starts:
             s = e - src_at
-            v = src[s : s + 12].reshape(12 * NY, NZ)
-            high = v.astype(BF16)
-            rest = (v - high.astype(F32)).astype(BF16)
-            along_z = jnp.dot(jnp.concatenate([high, rest], 1), cz_ref[...], preferred_element_type=F32)
-            along_z = along_z[:, :NZ] + along_z[:, NZ:]
-            along_y = []
             for i in range(0, 12, 2):
-                parts = [
-                    jnp.concatenate([a[NY * k : NY * k + NY] for a in (high, rest)], 0) for k in (i, i + 1)
-                ]
-                product = jnp.dot(cy_ref[...], jnp.concatenate(parts, 1), preferred_element_type=F32)
-                product = product[:NY] + product[NY:]
-                along_y += [product[:, :NZ], product[:, NZ:]]
+                v = src[pl.ds(s + i, 2)].reshape(2 * NY, NZ)
+                high = v.astype(BF16)
+                rest = (v - high.astype(F32)).astype(BF16)
+                along_z = jnp.dot(jnp.concatenate([high, rest], 1), cz_ref[...], preferred_element_type=F32)
+                along_z = along_z[:, :NZ] + along_z[:, NZ:]
+                parts = [jnp.concatenate([a[NY * k : NY * k + NY] for a in (high, rest)], 0) for k in range(2)]
+                along_y = jnp.dot(cy_ref[...], jnp.concatenate(parts, 1), preferred_element_type=F32)
+                along_y = along_y[:NY] + along_y[NY:]
+                for k in range(2):
+                    dst[e + i + k - dst_at] = along_z[NY * k : NY * k + NY] + along_y[:, NZ * k : NZ * k + NZ]
             for y in range(0, NY, 8):
                 window = [src[s - 6 + k, y : y + 8] for k in range(24)]
                 for i in range(12):
                     t = window[6 + i] * diag[e + i - 6, y : y + 8]
-                    t = t + (along_z[NY * i + y : NY * i + y + 8] + along_y[i][y : y + 8])
                     for m in range(1, 7):
                         t = t + WEIGHTS[m] * (window[6 + i + m] + window[6 + i - m])
+                    t = t + dst[e + i - dst_at, y : y + 8]
                     if prev is None:
                         t = t * 0.5
                     else:
                         t = t - prev[e + i - prev_at, y : y + 8]
-                    if e + i < 24:
+                    if masked and e + i < 24:
                         t = t * in_low
-                    elif e + i >= 48:
+                    elif masked and e + i >= 48:
                         t = t * in_high
                     dst[e + i - dst_at, y : y + 8] = t
 
@@ -216,12 +214,13 @@
             a0[12 * slab : 12 * slab + 12] = rb[o, slab].astype(F32) * (in_low if slab < 2 else in_high)
         a0[pl.ds(24 + 12 * other, 12)] = rb[o, 2 + other].astype(F32)
         a0[pl.ds(24 + 12 * h, 12)] = blkf[2 * h + o]
-        step(a0, 0, None, 0, a1, 6, 5)
-        step(a1, 6, a0, 0, a2, 12, 4)
-        step(a2, 12, a1, 6, a3, 18, 3)
-        step(a3, 18, a2, 12, a4.at[o], 24, 2)
+        step(a0, 0, None, 0, a1, 6, range(6, 66, 12))
+        step(a1, 6, a0, 0, a2, 12, range(12, 60, 12))
+        step(a2, 12, a1, 6, a3, 18, range(18, 54, 12))
+        step(a3, 18, a2, 12, a4.at[o], 24, (24 + 12 * other,), masked=False)
         sendp[o] = a4[o, pl.ds(12 * other, 12)].astype(BF16)
         start(gather(o)[:2])
+        step(a3, 18, a2, 12, a4.at[o], 24, (24 + 12 * h,), masked=False)
         low[group_low + o] = a4[o, pl.ds(12 * h, 12)].astype(BF16)
         start(gather(o)[2:])
         out_own(o).start()
@@ -262,6 +261,7 @@
     for piece in (third, second, first):
         total = total + lax.dot_general(fold, piece, (((1,), (1,)), ((), ())), preferred_element_type=F32)
 
+    sums = []
     for buffer, size, me, peer in ((ar1, 8, row, rowpeer), (ar2, 4, column, columnpeer)):
         part_at = part.at[0 if size == 8 else 1]
         part_at[...] = total
@@ -273,9 +273,10 @@
         total = buffer[0]
         for k in range(1, size):
             total = total + buffer[k]
-        sent(copies)
+        sums += copies
     inter[...] = total
 
+    sent(sums)
     sent(swap_pot + own_pot + forward_pot + share_pot)
     for o in range(2):
         sent(swap(o) + own(o) + forward(o) + gather(o) + relay(o))
@@ -317,7 +318,7 @@
             pltpu.SemaphoreType.DMA((44,)),
             pltpu.SemaphoreType.DMA((44,)),
         ],
-        compiler_params=pltpu.CompilerParams(collective_id=0, has_side_effects=True, vmem_limit_bytes=60 * 2**20),
+        compiler_params=pltpu.CompilerParams(collective_id=0, has_side_effects=True, vmem_limit_bytes=int(52.5 * 2**20)),
     )(block, potential, stored)
     return filtered, inter.T
 

time: 51.9 us -> 47.8 us (0.921)
  Pallas kernels: 47.6 us -> 44.1 us
  local copies, waits for them, and re-layouts: 3.36 us -> 2.4 us
    pallas_call x1, Pallas kernels: 47.6 us -> 44.1 us  [body(): pl.pallas_call(kernel, out_shape=(jax.ShapeDtypeStruct((4,) + planes, F32...]
    unnamed x2 -> x4, local copies, waits for them, and re-layouts: 3.36 us -> 2.4 us
where the time goes in v1:
time: 47.8 us; the launch traced here: 47.1 us
  Pallas kernels  44.1 us (92%)
  local copies, waits for them, and re-layouts  2.4 us (5%)
  between operations  0.65 us (1%)
    pallas_call x1, Pallas kernels, body(): pl.pallas_call(kernel, out_shape=(jax.ShapeDtypeStruct((4,) + planes, F32...  44.1 us
    unnamed x4, local copies, waits for them, and re-layouts  2.4 us

profile of v1, /device:TPU:0, one launch (start us, length us, event | category | flops | bytes accessed | tf_op | source)
XLA Modules:
  0.0 47.1 jit_solution(4329644872861633627)
XLA Ops:
  0.6 0.0 copy-start
  0.6 0.9 %copy-done = f32[12,32,128]{2,1,0:T(8,128)S(1)} copy-done((f32[12,32,128]{2,1,0:T(8,128)S(1)}, f32[12,32,128]{2,1,0:T(8,128)}, u32[]{:S(2)}) %copy-start) | copy-done | bytes 196632
  1.6 44.1 %shard_map.50 = (f32[4,12,32,128]{3,2,1,0:T(8,128)S(1)}, f32[16,64]{1,0:T(8,128)S(1)}) custom-call(f32[4,12,32,128]{3,2,1,0:T(8,128)} %block.1, f32[12,32,128]{2,1,0:T(8,128)S(1)} %copy-done, bf16[64,12,32,128]{3,2,1,0:T(8,128)(2,1)} %stored.1), custom_call_target="tpu_custom_call" | custom-call | tf_op jit(solution)/shard_map/pallas_call | solution.py:290
  45.7 0.9 %copy.7 = f32[4,12,32,128]{3,2,1,0:T(8,128)} copy(f32[4,12,32,128]{3,2,1,0:T(8,128)S(1)} %get-tuple-element.8) | data formatting | bytes 1572864
  46.5 0.6 %copy.8 = f32[64,16]{0,1:T(8,128)} copy(f32[64,16]{0,1:T(8,128)S(1)} %bitcast.1) | data formatting | bytes 8192
Async XLA Ops:
  0.6 0.9 %copy-start = (f32[12,32,128]{2,1,0:T(8,128)S(1)}, f32[12,32,128]{2,1,0:T(8,128)}, u32[]{:S(2)}) copy-start(f32[12,32,128]{2,1,0:T(8,128)} %potential.1) | copy-start | bytes 589828

commit v2 on v1

--- a/solution.py
+++ b/solution.py
@@ -185,11 +185,20 @@
                 along_y = along_y[:NY] + along_y[NY:]
                 for k in range(2):
                     dst[e + i + k - dst_at] = along_z[NY * k : NY * k + NY] + along_y[:, NZ * k : NZ * k + NZ]
+            for y in range(0, NY, 16):
+                window = [src[s - 6 + k, y : y + 16].astype(BF16) for k in range(24)]
+                for i in range(12):
+                    t = None
+                    for m in range(6, 2, -1):
+                        term = jnp.bfloat16(WEIGHTS[m]) * (window[6 + i + m] + window[6 + i - m])
+                        t = term if t is None else t + term
+                    at = e + i - dst_at
+                    dst[at, y : y + 16] = dst[at, y : y + 16] + t.astype(F32)
             for y in range(0, NY, 8):
                 window = [src[s - 6 + k, y : y + 8] for k in range(24)]
                 for i in range(12):
                     t = window[6 + i] * diag[e + i - 6, y : y + 8]
-                    for m in range(1, 7):
+                    for m in range(1, 3):
                         t = t + WEIGHTS[m] * (window[6 + i + m] + window[6 + i - m])
                     t = t + dst[e + i - dst_at, y : y + 8]
                     if prev is None:

time: 47.8 us -> 47.1 us (0.985)
  Pallas kernels: 44.1 us -> 43.4 us
    pallas_call x1, Pallas kernels: 44.1 us -> 43.4 us  [body(): pl.pallas_call(kernel, out_shape=(jax.ShapeDtypeStruct((4,) + planes, F32...]
where the time goes in v2:
time: 47.1 us; the launch traced here: 46.4 us
  Pallas kernels  43.4 us (92%)
  local copies, waits for them, and re-layouts  2.4 us (5%)
  between operations  0.65 us (1%)
    pallas_call x1, Pallas kernels, body(): pl.pallas_call(kernel, out_shape=(jax.ShapeDtypeStruct((4,) + planes, F32...  43.4 us
    unnamed x4, local copies, waits for them, and re-layouts  2.4 us

profile of v2, /device:TPU:0, one launch (start us, length us, event | category | flops | bytes accessed | tf_op | source)
XLA Modules:
  0.0 46.4 jit_solution(7307714325621242935)
XLA Ops:
  0.6 0.0 copy-start
  0.6 0.9 %copy-done = f32[12,32,128]{2,1,0:T(8,128)S(1)} copy-done((f32[12,32,128]{2,1,0:T(8,128)S(1)}, f32[12,32,128]{2,1,0:T(8,128)}, u32[]{:S(2)}) %copy-start) | copy-done | bytes 196632
  1.6 43.4 %shard_map.50 = (f32[4,12,32,128]{3,2,1,0:T(8,128)S(1)}, f32[16,64]{1,0:T(8,128)S(1)}) custom-call(f32[4,12,32,128]{3,2,1,0:T(8,128)} %block.1, f32[12,32,128]{2,1,0:T(8,128)S(1)} %copy-done, bf16[64,12,32,128]{3,2,1,0:T(8,128)(2,1)} %stored.1), custom_call_target="tpu_custom_call" | custom-call | tf_op jit(solution)/shard_map/pallas_call | solution.py:299
  45.0 0.9 %copy.7 = f32[4,12,32,128]{3,2,1,0:T(8,128)} copy(f32[4,12,32,128]{3,2,1,0:T(8,128)S(1)} %get-tuple-element.8) | data formatting | bytes 1572864
  45.8 0.6 %copy.8 = f32[64,16]{0,1:T(8,128)} copy(f32[64,16]{0,1:T(8,128)S(1)} %bitcast.1) | data formatting | bytes 8192
Async XLA Ops:
  0.6 0.9 %copy-start = (f32[12,32,128]{2,1,0:T(8,128)S(1)}, f32[12,32,128]{2,1,0:T(8,128)}, u32[]{:S(2)}) copy-start(f32[12,32,128]{2,1,0:T(8,128)} %potential.1) | copy-start | bytes 589828

commit v3 on v2

--- a/solution.py
+++ b/solution.py
@@ -80,10 +80,9 @@
     cz_ref[...] = jnp.concatenate([jnp.concatenate([high, rest], 1)] * 2, 0).astype(BF16)
     high, rest = circulant(NY, HIGHS), circulant(NY, LOWS)
     cy_ref[...] = jnp.concatenate([jnp.concatenate([high, high], 1), jnp.concatenate([rest, rest], 1)], 0).astype(BF16)
-    for load in loads:
+    for load in loads[:3]:
         load.wait()
-    load_stored.start()
-    for i in range(4):
+    for i in order[:2]:
         blkb[i] = blkf[i].astype(BF16)
     for r in range(2):
         potb[r, pl.ds(24 + 12 * h, 12)] = potf[:, 16 * r : 16 * r + 16].astype(BF16)
@@ -153,7 +152,13 @@
         for copy in copies:
             copy.wait_send()
 
-    start(swap_pot + own_pot + swap(0) + own(0))
+    start(swap_pot + swap(0) + own_pot)
+    for load in loads[3:]:
+        load.wait()
+    for i in order[2:]:
+        blkb[i] = blkf[i].astype(BF16)
+    start(own(0))
+    load_stored.start()
     received(swap_pot)
     start(forward_pot + swap(1))
     received(swap(0))

time: 47.1 us -> 47.1 us (level)
  no operation moved by 1% of the time
where the time goes in v3:
time: 47.1 us; the launch traced here: 46.4 us
  Pallas kernels  43.4 us (92%)
  local copies, waits for them, and re-layouts  2.4 us (5%)
  between operations  0.65 us (1%)
    pallas_call x1, Pallas kernels, body(): pl.pallas_call(kernel, out_shape=(jax.ShapeDtypeStruct((4,) + planes, F32...  43.4 us
    unnamed x4, local copies, waits for them, and re-layouts  2.4 us

profile of v3, /device:TPU:0, one launch (start us, length us, event | category | flops | bytes accessed | tf_op | source)
XLA Modules:
  0.0 46.4 jit_solution(15077004851070822510)
XLA Ops:
  0.6 0.0 copy-start
  0.6 0.9 %copy-done = f32[12,32,128]{2,1,0:T(8,128)S(1)} copy-done((f32[12,32,128]{2,1,0:T(8,128)S(1)}, f32[12,32,128]{2,1,0:T(8,128)}, u32[]{:S(2)}) %copy-start) | copy-done | bytes 196632
  1.6 43.4 %shard_map.50 = (f32[4,12,32,128]{3,2,1,0:T(8,128)S(1)}, f32[16,64]{1,0:T(8,128)S(1)}) custom-call(f32[4,12,32,128]{3,2,1,0:T(8,128)} %block.1, f32[12,32,128]{2,1,0:T(8,128)S(1)} %copy-done, bf16[64,12,32,128]{3,2,1,0:T(8,128)(2,1)} %stored.1), custom_call_target="tpu_custom_call" | custom-call | tf_op jit(solution)/shard_map/pallas_call | solution.py:304
  45.0 0.9 %copy.7 = f32[4,12,32,128]{3,2,1,0:T(8,128)} copy(f32[4,12,32,128]{3,2,1,0:T(8,128)S(1)} %get-tuple-element.8) | data formatting | bytes 1572864
  45.8 0.6 %copy.8 = f32[64,16]{0,1:T(8,128)} copy(f32[64,16]{0,1:T(8,128)S(1)} %bitcast.1) | data formatting | bytes 8192
Async XLA Ops:
  0.6 0.9 %copy-start = (f32[12,32,128]{2,1,0:T(8,128)S(1)}, f32[12,32,128]{2,1,0:T(8,128)}, u32[]{:S(2)}) copy-start(f32[12,32,128]{2,1,0:T(8,128)} %potential.1) | copy-start | bytes 589828
